TPU v7x, 32 devices: a whole 2x2x4 slice. The times are simulated.
32 devices in a mesh: blk: 8 (over z, y), group: 4 (over x, core).
Axes of the slice: x: 2, y: 2, z: 4, core: 2. Of those that a mesh axis runs over, the one named last changes fastest.
Arguments:
- image_embeds: bfloat16 [4, 768, 1152], P('group', 'blk')
- text_embeds: bfloat16 [4, 768, 1152], P('group', 'blk'), may hold values from -0.1875 to 0.1875
- positives: int32 [4, 768], P('group', 'blk'), may hold values from 0 to 767, each once within a row
- partner: int32 [4], replicated, may hold values from 0 to 3, each once
- log_temp: float32 [1], replicated, may hold values from 1.6 to 2.4
- bias: float32 [1], replicated, may hold values from -4 to -2
Outputs:
- image_grads: float32 [4, 768, 1152], P('group', 'blk')
- text_grads: float32 [4, 768, 1152], P('group', 'blk')
- loss: float32 [1], replicated
Inputs may be any that keep to these rules, and one draw needn't show every extreme that they name: Each group's positives name every text row of its partner group exactly once. `partner`: every group is named exactly once.
All inputs are finite; a program needn't handle non-finite values.
Results may differ from a plain program's by a relative error of at most 0.0015.
Values may be sent and summed in bfloat16 or wider, within the bound.
No kernel may reach another device: no remote copies, remote signals or barrier semaphores. Data moves between devices by JAX's collectives and lax.ppermute only.
A program may use at most 64 MiB of HBM per device.

v0:
```python
import functools

import jax
import jax.numpy as jnp
from jax import lax
from jax.experimental import pallas as pl
from jax.experimental.pallas import tpu as pltpu
from jax.sharding import PartitionSpec as P

TAIL = 16
DIGIT = 128


def pair_slopes(rows, others, hits, temper, offset):
    logits = temper * jnp.dot(rows, others.T, preferred_element_type=jnp.float32) + offset
    hit_values = hits.astype(jnp.float32)
    slopes = (jax.nn.sigmoid(logits) - hit_values).astype(jnp.bfloat16)
    return logits, hit_values, slopes


def exchange(array, axis, size, mate):
    return lax.ppermute(array, axis, [(place, mate(place)) for place in range(size)])


def swap(array, axis, size, bit):
    return exchange(array, axis, size, lambda place: place ^ bit)


def after(array, *earlier):
    return lax.optimization_barrier((array, *earlier))[0]


def entry(partner, group):
    lane = lax.broadcasted_iota(jnp.int32, partner.shape, 1)
    return jnp.sum(jnp.where(lane == group, partner[...], 0), axis=1, keepdims=True)


def position(partner, group):
    lane = lax.broadcasted_iota(jnp.int32, partner.shape, 1)
    return jnp.sum(jnp.where(partner[...] == group, lane, 0), axis=1, keepdims=True)


def same_chip(group, other):
    return (group ^ other) >> 1 == 0


def offer_kernel(partner, own, across, out):
    here = lax.axis_index("group")
    out[...] = jnp.where(same_chip(entry(partner, here ^ 1), here), own[...], across[...])


def choose_kernel(partner, own, across, offered, out):
    here = lax.axis_index("group")
    wanted = entry(partner, here)
    held = jnp.where(same_chip(wanted, here), own[...], across[...])
    out[...] = jnp.where((wanted ^ here) & 1 == 0, held, offered[...])


def scorer_kernel(partner, every, out):
    wanted = position(partner, lax.axis_index("group"))
    found = every[0]
    for group in range(1, every.shape[0]):
        found = jnp.where(wanted == group, every[group], found)
    out[...] = found


LINE = (0, 4, 2, 6)


def with_labels(images, labels):
    digits = jnp.stack([labels // DIGIT, labels % DIGIT]).astype(images.dtype)
    return jnp.concatenate([images, jnp.pad(digits, ((0, TAIL - 2), (0, images.shape[1] - labels.shape[0])))])


def labels_of(block, rows):
    digits = block[rows : rows + TAIL, :rows].astype(jnp.int32)
    return digits[:1] * DIGIT + digits[1:2]


def rows_by_rows(left, right):
    return lax.dot_general(left, right, (((1,), (1,)), ((), ())), preferred_element_type=jnp.float32)


def columns_by_rows(left, right):
    return lax.dot_general(left, right, (((0,), (0,)), ((), ())), preferred_element_type=jnp.float32)


def slopes_and_loss(products, temper, offset, hits):
    logits = temper * products + offset
    hit_values = hits.astype(jnp.float32)
    losses = jnp.maximum(logits, 0.0) + jnp.log1p(jnp.exp(-jnp.abs(logits))) - hit_values * logits
    return (jax.nn.sigmoid(logits) - hit_values).astype(jnp.bfloat16), losses


def image_kernel(log_temp, bias, images, mate, *refs):
    texts, (own_part, mate_part, loss) = refs[:-3], refs[-3:]
    rows = texts[0].shape[0]
    temper = jnp.exp(log_temp[...])
    offset = bias[...]
    place = lax.axis_index("blk")
    loss[...] = jnp.zeros_like(loss)
    for block, part in ((mate, mate_part), (images, own_part)):
        labels = labels_of(block, rows)
        total = jnp.zeros((rows, block.shape[1]), jnp.float32)
        for flip, some_texts in zip(LINE, texts):
            index = (place ^ flip) * rows + lax.broadcasted_iota(jnp.int32, (rows, rows), 0)
            products = rows_by_rows(some_texts[...], block[:rows, :])
            slopes, losses = slopes_and_loss(products, temper, offset, index == labels)
            loss[:, :rows] += losses.reshape(rows // 8, 8, rows).sum(axis=0)
            total += columns_by_rows(slopes, some_texts[...])
        part[...] = temper * total


def text_kernel(flip, log_temp, bias, texts, *refs):
    images, part = refs[:-1], refs[-1]
    rows = texts.shape[0]
    temper = jnp.exp(log_temp[...])
    index = (lax.axis_index("blk") ^ flip) * rows + lax.broadcasted_iota(jnp.int32, (rows, rows), 0)
    total = jnp.zeros(part.shape, jnp.float32)
    for block in images:
        products = rows_by_rows(texts[...], block[:rows, :])
        slopes, _ = slopes_and_loss(products, temper, bias[...], index == labels_of(block, rows))
        total += jnp.dot(slopes, block[:rows, :], preferred_element_type=jnp.float32)
    part[...] = temper * total


def call(kernel, arrays, shapes, name, dtype=jnp.float32):
    return pl.pallas_call(
        kernel,
        out_shape=[jax.ShapeDtypeStruct(shape, dtype) for shape in shapes],
        in_specs=[pl.BlockSpec(memory_space=pltpu.VMEM)] * len(arrays),
        out_specs=[pl.BlockSpec(memory_space=pltpu.VMEM)] * len(shapes),
        compiler_params=pltpu.CompilerParams(vmem_limit_bytes=16 * 2**20),
        name=name,
    )(*arrays)


def hop_sum(total, hops):
    for axis, size, bit in hops:
        total = total + swap(total, axis, size, bit)
    return total


def shards(image_embeds, text_embeds, positives, partner, log_temp, bias):
    texts = text_embeds[0]
    labels = positives[0]
    rows = texts.shape[0]
    blocks = lax.axis_size("blk")
    groups = lax.axis_size("group")
    blk_place = lax.axis_index("blk")
    images = with_labels(image_embeds[0], labels)

    def index_of(places):
        return (jnp.stack(places)[:, None] * rows + jnp.arange(rows)[None, :]).reshape(-1)

    def matches(some_labels, index):
        return some_labels[:, None] == index[None, :]

    def grads(slopes, others):
        return temper * jnp.dot(slopes, others, preferred_element_type=jnp.float32)

    packed = after(jnp.concatenate([images, texts]))
    tailed = images.shape[0]
    own_images, own_texts = packed[:rows], packed[tailed:]
    hops = [("blk", blocks, 1)] + [("group", groups, 1 << step) for step in range(groups.bit_length() - 1)]
    hops += [("blk", blocks, 1 << step) for step in range(1, blocks.bit_length() - 1)]
    choice = partner.reshape(1, groups)
    texts_across = swap(texts, "group", groups, 2)
    offer = call(offer_kernel, [choice, own_texts, texts_across], [texts.shape], "offer", texts.dtype)[0]
    offered = swap(offer, "group", groups, 1)
    partner_text = call(choose_kernel, [choice, own_texts, texts_across, offered], [texts.shape], "choose", texts.dtype)[0]
    group_images = lax.all_gather(after(packed[:tailed], partner_text), "group")
    scorer_image = call(scorer_kernel, [choice, group_images], [images.shape], "scorer", images.dtype)[0]

    if blocks == 8:

        def along(array, flip):
            return swap(array, "blk", blocks, flip)

        mate = along(packed, 1)
        text_two_off = along(partner_text, 4)
        text_one_off = along(partner_text, 2)
        text_three_off = along(after(text_two_off, text_one_off, mate, scorer_image), 2)
        image_two_off = along(scorer_image, 4)
        image_one_off = along(after(scorer_image, text_three_off), 2)
        column_texts = [partner_text, text_two_off, text_one_off, after(text_three_off, image_two_off)]
        scalars = (log_temp.reshape(1, 1), bias.reshape(1, 1))
        block_shape = texts.shape
        own_part, mate_part, total = call(
            image_kernel, [*scalars, packed[:tailed], mate[:tailed], *column_texts], [block_shape, block_shape, (8, 128)], "image_side"
        )
        image_three_off = along(after(image_two_off, image_one_off, total), 2)
        image_grads = own_part + along(mate_part, 1)
        total = hop_sum(total, hops[:2])
        column_images = [scorer_image, image_two_off, image_one_off, after(image_three_off, total)]
        mate_part = call(functools.partial(text_kernel, 1), [*scalars, mate[tailed:], *column_images], [block_shape], "text_side_mate")[0]
        own_part = call(functools.partial(text_kernel, 0), [*scalars, own_texts, *column_images], [block_shape], "text_side_own")[0]
        text_grads = own_part + along(mate_part, 1)
        total = after(total, image_grads)
    else:
        temper = jnp.exp(log_temp[0])
        offset = bias[0]
        all_texts = lax.all_gather(partner_text, "blk", axis=0, tiled=True)
        every_image = lax.all_gather(scorer_image, "blk", axis=0)
        hits = matches(labels, jnp.arange(blocks * rows))
        logits, hit_values, slopes = pair_slopes(own_images, all_texts, hits, temper, offset)
        total = jnp.sum(jax.nn.softplus(logits) - hit_values * logits)
        total = hop_sum(jnp.zeros((8, 128)).at[0, 0].set(total), hops[:2])
        image_grads = grads(slopes, all_texts)
        all_images = every_image[:, :rows].reshape(blocks * rows, -1)
        back_labels = jax.vmap(lambda block: labels_of(block, rows)[0])(every_image).reshape(-1)
        back_hits = matches(index_of([blk_place]), back_labels)
        back_slopes = pair_slopes(own_texts, all_images, back_hits, temper, offset)[2]
        text_grads = grads(back_slopes, all_images)

    total = hop_sum(total, hops[2:])
    loss = jnp.sum(total).reshape(1) / (groups * rows * blocks * blocks)
    return (image_grads[None], text_grads[None], loss)


def solution(mesh):
    in_specs = (P("group", "blk", None), P("group", "blk", None), P("group", "blk"), P(), P(), P())
    out_specs = (P("group", "blk", None), P("group", "blk", None), P())
    return jax.shard_map(shards, mesh=mesh, in_specs=in_specs, out_specs=out_specs, check_vma=False)
```

profile of v0, /device:TPU:0, one launch (start us, length us, event | category | flops | bytes accessed | tf_op | source)
XLA Modules:
  0.0 79.4 jit_solution(5786516315445115194)
XLA Ops:
  0.6 0.0 copy-start.1
  0.6 3.0 %collective-permute-start.1 = (bf16[96,1152]{1,0:T(8,128)(2,1)}, bf16[96,1152]{1,0:T(8,128)(2,1)S(1)}, u32[]{:S(2)}, u32[]{:S(2)}) collective-permute-start(bf16[96,1152]{1,0:T(8,128)(2,1)} %bitcast.22), channel_id=1, source_target_pairs={{0,2},{1,3},{2,0},{3,1},{4,6},{5,7},{6,4},{7,5},{8,10},{9,11},{10,... | collective-permute-start | bytes 663560 | tf_op jit(solution)/shard_map/ppermute | solution.py:22
  3.6 0.0 copy-done.1
  3.7 1.1 %pad_maximum_fusion = bf16[208,1152]{1,0:T(8,128)(2,1)S(1)} fusion(bf16[96,1152]{1,0:T(8,128)(2,1)} %bitcast.23, bf16[16,1152]{1,0:T(8,128)(2,1)S(1)} %fusion.5, bf16[96,1152]{1,0:T(8,128)(2,1)} %bitcast.21), kind=kLoop, calls=%fused_computation | loop fusion | flops 1437696 | bytes 958464 | tf_op jit(solution)/shard_map/concatenate | solution.py:162
  4.8 0.0 copy-start
  4.8 4.5 %collective-permute-done.1.across = bf16[96,1152]{1,0:T(8,128)(2,1)S(1)} collective-permute-done((bf16[96,1152]{1,0:T(8,128)(2,1)}, bf16[96,1152]{1,0:T(8,128)(2,1)S(1)}, u32[]{:S(2)}, u32[]{:S(2)}) %collective-permute-start.1) | collective-permute-done | bytes 221216 | tf_op jit(solution)/shard_map/ppermute | solution.py:22
  9.3 0.0 copy-done
  9.3 0.1 offer.1
  9.4 0.1 collective-permute-start.2
  9.5 1.8 %collective-permute-start = (bf16[208,1152]{1,0:T(8,128)(2,1)S(1)}, bf16[208,1152]{1,0:T(8,128)(2,1)S(1)}, u32[]{:S(2)}, u32[]{:S(2)}) collective-permute-start(bf16[208,1152]{1,0:T(8,128)(2,1)S(1)} %pad_maximum_fusion), channel_id=1, source_target_pairs={{0,4},{4,0},{8,12},{12,8},{16,20},{20,16},{24,28},{28,24},{1,5},{5... | collective-permute-start | bytes 1437704 | tf_op jit(solution)/shard_map/ppermute | solution.py:22
  11.3 0.0 collective-permute-done.2.offered
  11.4 0.1 choose.1.refs_0_
  11.5 1.6 %collective-permute-start.4 = (bf16[96,1152]{1,0:T(8,128)(2,1)S(1)}, bf16[96,1152]{1,0:T(8,128)(2,1)S(1)}, u32[]{:S(2)}, u32[]{:S(2)}) collective-permute-start(bf16[96,1152]{1,0:T(8,128)(2,1)S(1)} %choose.1.refs_0_), channel_id=1, source_target_pairs={{0,8},{4,12},{8,0},{12,4},{16,24},{20,28},{24,16},{28,20},{1,9},{5... | collective-permute-start | bytes 663560 | tf_op jit(solution)/shard_map/ppermute | solution.py:22
  13.1 2.6 %collective-permute-start.3 = (bf16[96,1152]{1,0:T(8,128)(2,1)S(1)}, bf16[96,1152]{1,0:T(8,128)(2,1)S(1)}, u32[]{:S(2)}, u32[]{:S(2)}) collective-permute-start(bf16[96,1152]{1,0:T(8,128)(2,1)S(1)} %choose.1.refs_0_), channel_id=1, source_target_pairs={{0,16},{4,20},{8,24},{12,28},{16,0},{20,4},{24,8},{28,12},{1,17},{... | collective-permute-start | bytes 663560 | tf_op jit(solution)/shard_map/ppermute | solution.py:22
  15.7 9.9 %all-gather = bf16[448,1152]{1,0:T(8,128)(2,1)S(1)} all-gather(bf16[112,1152]{1,0:T(8,128)(2,1)S(1)} %slice.17.images), channel_id=2, replica_groups=mesh['blk'=8,'group'=4] {'group'}, dimensions={0}, use_global_device_ids=true | all-gather | bytes 1290240 | tf_op jit(solution)/shard_map/all_gather | solution.py:172
  25.6 0.2 scorer.1.refs_0_
  25.8 0.0 collective-permute-done
  25.8 0.0 collective-permute-done.4.refs_2_
  25.8 0.2 collective-permute-done.3.refs_1_
  26.0 0.4 collective-permute-start.5
  26.5 2.6 %collective-permute-start.6 = (bf16[112,1152]{1,0:T(8,128)(2,1)S(1)}, bf16[112,1152]{1,0:T(8,128)(2,1)S(1)}, u32[]{:S(2)}, u32[]{:S(2)}) collective-permute-start(bf16[112,1152]{1,0:T(8,128)(2,1)S(1)} %scorer.1.refs_0_), channel_id=1, source_target_pairs={{0,16},{4,20},{8,24},{12,28},{16,0},{20,4},{24,8},{28,12},{1,17},{... | collective-permute-start | bytes 774152 | tf_op jit(solution)/shard_map/ppermute | solution.py:22
  29.1 8.0 %collective-permute-done.5.refs_3_ = bf16[96,1152]{1,0:T(8,128)(2,1)S(1)} collective-permute-done((bf16[96,1152]{1,0:T(8,128)(2,1)S(1)}, bf16[96,1152]{1,0:T(8,128)(2,1)S(1)}, u32[]{:S(2)}, u32[]{:S(2)}) %collective-permute-start.5) | collective-permute-done | bytes 221216 | tf_op jit(solution)/shard_map/ppermute | solution.py:22
  37.1 0.0 collective-permute-start.8
  38.4 2.7 %collective-permute-done.6.refs_1_ = bf16[112,1152]{1,0:T(8,128)(2,1)S(1)} collective-permute-done((bf16[112,1152]{1,0:T(8,128)(2,1)S(1)}, bf16[112,1152]{1,0:T(8,128)(2,1)S(1)}, u32[]{:S(2)}, u32[]{:S(2)}) %collective-permute-start.6) | collective-permute-done | bytes 258080 | tf_op jit(solution)/shard_map/ppermute | solution.py:22
  41.1 2.6 %image_side.1 = (f32[96,1152]{1,0:T(8,128)S(1)}, f32[96,1152]{1,0:T(8,128)S(1)}, f32[8,128]{1,0:T(8,128)S(1)}) custom-call(f32[1,1]{1,0:T(1,128)} %bitcast.10.log_temp, f32[1,1]{1,0:T(1,128)} %bitcast.13.bias, bf16[112,1152]{1,0:T(8,128)(2,1)S(1)} %slice.17.images, bf16[112,1152]{1,0:T(8,128)(2,1)S(1)} %slice.18.mate, bf16[96,1152]{1,0:T(8,128)(2,1)S(1)} %choose.1.refs_0_, ...), custom_call_target="tpu_custom_call" | custom-call | tf_op jit(solution)/shard_map/image_side/pallas_call | solution.py:128
  43.7 2.9 %collective-permute-done.8.refs_2_ = bf16[112,1152]{1,0:T(8,128)(2,1)S(1)} collective-permute-done((bf16[112,1152]{1,0:T(8,128)(2,1)S(1)}, bf16[112,1152]{1,0:T(8,128)(2,1)S(1)}, u32[]{:S(2)}, u32[]{:S(2)}) %collective-permute-start.8) | collective-permute-done | bytes 258080 | tf_op jit(solution)/shard_map/ppermute | solution.py:22
  46.6 0.0 collective-permute-start.9
  46.6 1.4 %collective-permute-start.7 = (f32[96,1152]{1,0:T(8,128)S(1)}, f32[96,1152]{1,0:T(8,128)S(1)}, u32[]{:S(2)}, u32[]{:S(2)}) collective-permute-start(f32[96,1152]{1,0:T(8,128)S(1)} %get-tuple-element.17), channel_id=1, source_target_pairs={{0,4},{4,0},{8,12},{12,8},{16,20},{20,16},{24,28},{28,24},{1,5},{5... | collective-permute-start | bytes 1327112 | tf_op jit(solution)/shard_map/ppermute | solution.py:22
  47.9 0.7 collective-permute-start.10
  48.6 10.2 %collective-permute-done.10 = f32[8,128]{1,0:T(8,128)S(1)} collective-permute-done((f32[8,128]{1,0:T(8,128)S(1)}, f32[8,128]{1,0:T(8,128)S(1)}, u32[]{:S(2)}, u32[]{:S(2)}) %collective-permute-start.10) | collective-permute-done | bytes 4128 | tf_op jit(solution)/shard_map/ppermute | solution.py:22
  58.7 0.0 collective-permute-start.11
  58.8 1.1 %collective-permute-done.11 = f32[8,128]{1,0:T(8,128)S(1)} collective-permute-done((f32[8,128]{1,0:T(8,128)S(1)}, f32[8,128]{1,0:T(8,128)S(1)}, u32[]{:S(2)}, u32[]{:S(2)}) %collective-permute-start.11) | collective-permute-done | bytes 4128 | tf_op jit(solution)/shard_map/ppermute | solution.py:22
  59.9 0.0 collective-permute-done.9.refs_3_
  59.9 1.1 %text_side_mate.1 = f32[96,1152]{1,0:T(8,128)S(1)} custom-call(f32[1,1]{1,0:T(1,128)} %bitcast.12.log_temp, f32[1,1]{1,0:T(1,128)} %bitcast.15.bias, bf16[96,1152]{1,0:T(8,128)(2,1)S(1)} %slice.20.texts, bf16[112,1152]{1,0:T(8,128)(2,1)S(1)} %scorer.1.refs_0_, bf16[112,1152]{1,0:T(8,128)(2,1)S(1)} %collective-permute-done.6.refs_1_, ...), custom_call_target="tpu_custom_call" | custom-call | tf_op jit(solution)/shard_map/text_side_mate/pallas_call | solution.py:128
  61.1 1.4 %collective-permute-start.12 = (f32[96,1152]{1,0:T(8,128)S(1)}, f32[96,1152]{1,0:T(8,128)S(1)}, u32[]{:S(2)}, u32[]{:S(2)}) collective-permute-start(f32[96,1152]{1,0:T(8,128)S(1)} %text_side_mate.1), channel_id=1, source_target_pairs={{0,4},{4,0},{8,12},{12,8},{16,20},{20,16},{24,28},{28,24},{1,5},{5... | collective-permute-start | bytes 1327112 | tf_op jit(solution)/shard_map/ppermute | solution.py:22
  62.5 0.0 collective-permute-done.7
  62.5 0.8 %add.33 = f32[96,1152]{1,0:T(8,128)} add(f32[96,1152]{1,0:T(8,128)S(1)} %get-tuple-element.16, f32[96,1152]{1,0:T(8,128)S(1)} %collective-permute-done.7) | non-fusion elementwise | flops 110592 | bytes 1327104 | tf_op jit(solution)/shard_map/add | solution.py:193
  63.3 0.0 collective-permute-start.13
  63.3 3.6 %collective-permute-done.13 = f32[8,128]{1,0:T(8,128)S(1)} collective-permute-done((f32[8,128]{1,0:T(8,128)S(1)}, f32[8,128]{1,0:T(8,128)S(1)}, u32[]{:S(2)}, u32[]{:S(2)}) %collective-permute-start.13) | collective-permute-done | bytes 4128 | tf_op jit(solution)/shard_map/ppermute | solution.py:22
  66.9 1.7 %collective-permute-start.14 = (f32[8,128]{1,0:T(8,128)S(1)}, f32[8,128]{1,0:T(8,128)S(1)}, u32[]{:S(2)}, u32[]{:S(2)}) collective-permute-start(f32[8,128]{1,0:T(8,128)S(1)} %add.37), channel_id=1, source_target_pairs={{0,8},{4,12},{8,0},{12,4},{16,24},{20,28},{24,16},{28,20},{1,9},{5... | collective-permute-start | bytes 12296 | tf_op jit(solution)/shard_map/ppermute | solution.py:22
  68.7 1.9 %collective-permute-done.14 = f32[8,128]{1,0:T(8,128)S(1)} collective-permute-done((f32[8,128]{1,0:T(8,128)S(1)}, f32[8,128]{1,0:T(8,128)S(1)}, u32[]{:S(2)}, u32[]{:S(2)}) %collective-permute-start.14) | collective-permute-done | bytes 4128 | tf_op jit(solution)/shard_map/ppermute | solution.py:22
  70.6 0.0 collective-permute-start.15
  70.6 4.5 %collective-permute-done.15 = f32[8,128]{1,0:T(8,128)S(1)} collective-permute-done((f32[8,128]{1,0:T(8,128)S(1)}, f32[8,128]{1,0:T(8,128)S(1)}, u32[]{:S(2)}, u32[]{:S(2)}) %collective-permute-start.15) | collective-permute-done | bytes 4128 | tf_op jit(solution)/shard_map/ppermute | solution.py:22
  75.1 0.6 add_reduce_fusion
  76.3 1.1 %text_side_own.1 = f32[96,1152]{1,0:T(8,128)S(1)} custom-call(f32[1,1]{1,0:T(1,128)} %bitcast.11.log_temp, f32[1,1]{1,0:T(1,128)} %bitcast.14.bias, bf16[96,1152]{1,0:T(8,128)(2,1)S(1)} %slice.19.own.texts, bf16[112,1152]{1,0:T(8,128)(2,1)S(1)} %scorer.1.refs_0_, bf16[112,1152]{1,0:T(8,128)(2,1)S(1)} %collective-permute-done.6.refs_1_, ...), custom_call_target="tpu_custom_call" | custom-call | tf_op jit(solution)/shard_map/text_side_own/pallas_call | solution.py:128
  77.5 0.0 collective-permute-done.12
  77.5 0.8 %add_bitcast_fusion = f32[1,96,1152]{2,1,0:T(8,128)} fusion(f32[96,1152]{1,0:T(8,128)S(1)} %text_side_own.1, f32[96,1152]{1,0:T(8,128)S(1)} %collective-permute-done.12), kind=kLoop, calls=%fused_computation.1 | loop fusion | flops 110592 | bytes 1327104 | tf_op jit(solution)/shard_map/broadcast_in_dim | solution.py:218
  (10 shorter events, 0.1 us)
Async XLA Ops:
  0.6 3.0 %copy-start.1 = (s32[1,96]{1,0:T(1,128)S(1)}, s32[1,96]{1,0:T(1,128)}, u32[]{:S(2)}) copy-start(s32[1,96]{1,0:T(1,128)} %param.8) | copy-start | bytes 1156
  0.6 8.6 %collective-permute-start.1 = (bf16[96,1152]{1,0:T(8,128)(2,1)}, bf16[96,1152]{1,0:T(8,128)(2,1)S(1)}, u32[]{:S(2)}, u32[]{:S(2)}) collective-permute-start(bf16[96,1152]{1,0:T(8,128)(2,1)} %bitcast.22), channel_id=1, source_target_pairs={{0,2},{1,3},{2,0},{3,1},{4,6},{5,7},{6,4},{7,5},{8,10},{9,11},{10,... | collective-permute-start | bytes 663560 | tf_op jit(solution)/shard_map/ppermute | solution.py:22
  4.8 4.5 %copy-start = (s32[4]{0:T(128)S(1)}, s32[4]{0:T(128)}, u32[]{:S(2)}) copy-start(s32[4]{0:T(128)} %param.9) | copy-start | bytes 52
  9.4 1.9 %collective-permute-start.2 = (bf16[96,1152]{1,0:T(8,128)(2,1)S(1)}, bf16[96,1152]{1,0:T(8,128)(2,1)S(1)}, u32[]{:S(2)}, u32[]{:S(2)}) collective-permute-start(bf16[96,1152]{1,0:T(8,128)(2,1)S(1)} %offer.1), channel_id=1, source_target_pairs={{0,1},{1,0},{2,3},{3,2},{4,5},{5,4},{6,7},{7,6},{8,9},{9,8},{10,11... | collective-permute-start | bytes 663560 | tf_op jit(solution)/shard_map/ppermute | solution.py:22
  9.5 16.3 %collective-permute-start = (bf16[208,1152]{1,0:T(8,128)(2,1)S(1)}, bf16[208,1152]{1,0:T(8,128)(2,1)S(1)}, u32[]{:S(2)}, u32[]{:S(2)}) collective-permute-start(bf16[208,1152]{1,0:T(8,128)(2,1)S(1)} %pad_maximum_fusion), channel_id=1, source_target_pairs={{0,4},{4,0},{8,12},{12,8},{16,20},{20,16},{24,28},{28,24},{1,5},{5... | collective-permute-start | bytes 1437704 | tf_op jit(solution)/shard_map/ppermute | solution.py:22
  11.5 14.3 %collective-permute-start.4 = (bf16[96,1152]{1,0:T(8,128)(2,1)S(1)}, bf16[96,1152]{1,0:T(8,128)(2,1)S(1)}, u32[]{:S(2)}, u32[]{:S(2)}) collective-permute-start(bf16[96,1152]{1,0:T(8,128)(2,1)S(1)} %choose.1.refs_0_), channel_id=1, source_target_pairs={{0,8},{4,12},{8,0},{12,4},{16,24},{20,28},{24,16},{28,20},{1,9},{5... | collective-permute-start | bytes 663560 | tf_op jit(solution)/shard_map/ppermute | solution.py:22
  13.1 12.9 %collective-permute-start.3 = (bf16[96,1152]{1,0:T(8,128)(2,1)S(1)}, bf16[96,1152]{1,0:T(8,128)(2,1)S(1)}, u32[]{:S(2)}, u32[]{:S(2)}) collective-permute-start(bf16[96,1152]{1,0:T(8,128)(2,1)S(1)} %choose.1.refs_0_), channel_id=1, source_target_pairs={{0,16},{4,20},{8,24},{12,28},{16,0},{20,4},{24,8},{28,12},{1,17},{... | collective-permute-start | bytes 663560 | tf_op jit(solution)/shard_map/ppermute | solution.py:22
  26.0 11.1 %collective-permute-start.5 = (bf16[96,1152]{1,0:T(8,128)(2,1)S(1)}, bf16[96,1152]{1,0:T(8,128)(2,1)S(1)}, u32[]{:S(2)}, u32[]{:S(2)}) collective-permute-start(bf16[96,1152]{1,0:T(8,128)(2,1)S(1)} %collective-permute-done.3.refs_1_), channel_id=1, source_target_pairs={{0,8},{4,12},{8,0},{12,4},{16,24},{20,28},{24,16},{28,20},{1,9},{5... | collective-permute-start | bytes 663560 | tf_op jit(solution)/shard_map/ppermute | solution.py:22
  26.5 14.6 %collective-permute-start.6 = (bf16[112,1152]{1,0:T(8,128)(2,1)S(1)}, bf16[112,1152]{1,0:T(8,128)(2,1)S(1)}, u32[]{:S(2)}, u32[]{:S(2)}) collective-permute-start(bf16[112,1152]{1,0:T(8,128)(2,1)S(1)} %scorer.1.refs_0_), channel_id=1, source_target_pairs={{0,16},{4,20},{8,24},{12,28},{16,0},{20,4},{24,8},{28,12},{1,17},{... | collective-permute-start | bytes 774152 | tf_op jit(solution)/shard_map/ppermute | solution.py:22
  37.1 9.5 %collective-permute-start.8 = (bf16[112,1152]{1,0:T(8,128)(2,1)S(1)}, bf16[112,1152]{1,0:T(8,128)(2,1)S(1)}, u32[]{:S(2)}, u32[]{:S(2)}) collective-permute-start(bf16[112,1152]{1,0:T(8,128)(2,1)S(1)} %scorer.1.refs_0_), channel_id=1, source_target_pairs={{0,8},{4,12},{8,0},{12,4},{16,24},{20,28},{24,16},{28,20},{1,9},{5... | collective-permute-start | bytes 774152 | tf_op jit(solution)/shard_map/ppermute | solution.py:22
  46.6 13.4 %collective-permute-start.9 = (bf16[112,1152]{1,0:T(8,128)(2,1)S(1)}, bf16[112,1152]{1,0:T(8,128)(2,1)S(1)}, u32[]{:S(2)}, u32[]{:S(2)}) collective-permute-start(bf16[112,1152]{1,0:T(8,128)(2,1)S(1)} %collective-permute-done.6.refs_1_), channel_id=1, source_target_pairs={{0,8},{4,12},{8,0},{12,4},{16,24},{20,28},{24,16},{28,20},{1,9},{5... | collective-permute-start | bytes 774152 | tf_op jit(solution)/shard_map/ppermute | solution.py:22
  46.6 15.9 %collective-permute-start.7 = (f32[96,1152]{1,0:T(8,128)S(1)}, f32[96,1152]{1,0:T(8,128)S(1)}, u32[]{:S(2)}, u32[]{:S(2)}) collective-permute-start(f32[96,1152]{1,0:T(8,128)S(1)} %get-tuple-element.17), channel_id=1, source_target_pairs={{0,4},{4,0},{8,12},{12,8},{16,20},{20,16},{24,28},{28,24},{1,5},{5... | collective-permute-start | bytes 1327112 | tf_op jit(solution)/shard_map/ppermute | solution.py:22
  47.9 10.8 %collective-permute-start.10 = (f32[8,128]{1,0:T(8,128)S(1)}, f32[8,128]{1,0:T(8,128)S(1)}, u32[]{:S(2)}, u32[]{:S(2)}) collective-permute-start(f32[8,128]{1,0:T(8,128)S(1)} %get-tuple-element.19), channel_id=1, source_target_pairs={{0,4},{4,0},{8,12},{12,8},{16,20},{20,16},{24,28},{28,24},{1,5},{5... | collective-permute-start | bytes 12296 | tf_op jit(solution)/shard_map/ppermute | solution.py:22
  58.7 1.2 %collective-permute-start.11 = (f32[8,128]{1,0:T(8,128)S(1)}, f32[8,128]{1,0:T(8,128)S(1)}, u32[]{:S(2)}, u32[]{:S(2)}) collective-permute-start(f32[8,128]{1,0:T(8,128)S(1)} %add.34), channel_id=1, source_target_pairs={{0,1},{1,0},{2,3},{3,2},{4,5},{5,4},{6,7},{7,6},{8,9},{9,8},{10,11... | collective-permute-start | bytes 12296 | tf_op jit(solution)/shard_map/ppermute | solution.py:22
  61.1 16.4 %collective-permute-start.12 = (f32[96,1152]{1,0:T(8,128)S(1)}, f32[96,1152]{1,0:T(8,128)S(1)}, u32[]{:S(2)}, u32[]{:S(2)}) collective-permute-start(f32[96,1152]{1,0:T(8,128)S(1)} %text_side_mate.1), channel_id=1, source_target_pairs={{0,4},{4,0},{8,12},{12,8},{16,20},{20,16},{24,28},{28,24},{1,5},{5... | collective-permute-start | bytes 1327112 | tf_op jit(solution)/shard_map/ppermute | solution.py:22
  63.3 3.6 %collective-permute-start.13 = (f32[8,128]{1,0:T(8,128)S(1)}, f32[8,128]{1,0:T(8,128)S(1)}, u32[]{:S(2)}, u32[]{:S(2)}) collective-permute-start(f32[8,128]{1,0:T(8,128)S(1)} %add.35), channel_id=1, source_target_pairs={{0,2},{1,3},{2,0},{3,1},{4,6},{5,7},{6,4},{7,5},{8,10},{9,11},{10,... | collective-permute-start | bytes 12296 | tf_op jit(solution)/shard_map/ppermute | solution.py:22
  66.9 3.6 %collective-permute-start.14 = (f32[8,128]{1,0:T(8,128)S(1)}, f32[8,128]{1,0:T(8,128)S(1)}, u32[]{:S(2)}, u32[]{:S(2)}) collective-permute-start(f32[8,128]{1,0:T(8,128)S(1)} %add.37), channel_id=1, source_target_pairs={{0,8},{4,12},{8,0},{12,4},{16,24},{20,28},{24,16},{28,20},{1,9},{5... | collective-permute-start | bytes 12296 | tf_op jit(solution)/shard_map/ppermute | solution.py:22
  70.6 4.5 %collective-permute-start.15 = (f32[8,128]{1,0:T(8,128)S(1)}, f32[8,128]{1,0:T(8,128)S(1)}, u32[]{:S(2)}, u32[]{:S(2)}) collective-permute-start(f32[8,128]{1,0:T(8,128)S(1)} %add.38), channel_id=1, source_target_pairs={{0,16},{4,20},{8,24},{12,28},{16,0},{20,4},{24,8},{28,12},{1,17},{... | collective-permute-start | bytes 12296 | tf_op jit(solution)/shard_map/ppermute | solution.py:22
where the time goes:
time: 79.6 us; the launch traced here: 79.4 us
  waiting for transfers between devices  39.6 us (50%)
  starting transfers between devices  17.4 us (22%)
  blocking collectives  9.92 us (12%)
  Pallas kernels  5.26 us (7%)
  between operations  3.85 us (5%)
  other arithmetic  3.37 us (4%)
    ppermute x16, waiting for transfers between devices, exchange(): lax.ppermute(array, axis, [(place, mate(place)) for place in range(size)])  39.6 us
    ppermute x16, starting transfers between devices, exchange(): lax.ppermute(array, axis, [(place, mate(place)) for place in range(size)])  17.4 us
    all_gather x1, blocking collectives, shards(): group_images = lax.all_gather(after(packed[:tailed], partner_text), 'group')  9.92 us
    pallas_call x6, Pallas kernels, call(): pl.pallas_call(kernel, out_shape=[jax.ShapeDtypeStruct(shape, dtype) for...  5.26 us
  transfers between devices with their start and end apart: 16, of which 10 were waited for; matrix products, arithmetic and copies ran while one was open for 3% of the time, Pallas kernels for 6%

commit v1 on v0

--- a/solution.py
+++ b/solution.py
@@ -92,34 +92,32 @@
     return (jax.nn.sigmoid(logits) - hit_values).astype(jnp.bfloat16), losses
 
 
-def image_kernel(log_temp, bias, images, mate, *refs):
-    texts, (own_part, mate_part, loss) = refs[:-3], refs[-3:]
+def image_kernel(settings, images, *refs):
+    texts, (part, loss) = refs[:-2], refs[-2:]
     rows = texts[0].shape[0]
-    temper = jnp.exp(log_temp[...])
-    offset = bias[...]
+    temper = jnp.exp(settings[:, :1])
     place = lax.axis_index("blk")
+    labels = labels_of(images, rows)
     loss[...] = jnp.zeros_like(loss)
-    for block, part in ((mate, mate_part), (images, own_part)):
-        labels = labels_of(block, rows)
-        total = jnp.zeros((rows, block.shape[1]), jnp.float32)
-        for flip, some_texts in zip(LINE, texts):
-            index = (place ^ flip) * rows + lax.broadcasted_iota(jnp.int32, (rows, rows), 0)
-            products = rows_by_rows(some_texts[...], block[:rows, :])
-            slopes, losses = slopes_and_loss(products, temper, offset, index == labels)
-            loss[:, :rows] += losses.reshape(rows // 8, 8, rows).sum(axis=0)
-            total += columns_by_rows(slopes, some_texts[...])
-        part[...] = temper * total
-
-
-def text_kernel(flip, log_temp, bias, texts, *refs):
+    total = jnp.zeros(part.shape, jnp.float32)
+    for flip, some_texts in zip(LINE, texts):
+        index = (place ^ flip) * rows + lax.broadcasted_iota(jnp.int32, (rows, rows), 0)
+        products = rows_by_rows(some_texts[...], images[:rows, :])
+        slopes, losses = slopes_and_loss(products, temper, settings[:, 1:2], index == labels)
+        loss[:, :rows] += losses.reshape(rows // 8, 8, rows).sum(axis=0)
+        total += columns_by_rows(slopes, some_texts[...])
+    part[...] = temper * total
+
+
+def text_kernel(flip, settings, texts, *refs):
     images, part = refs[:-1], refs[-1]
     rows = texts.shape[0]
-    temper = jnp.exp(log_temp[...])
+    temper = jnp.exp(settings[:, :1])
     index = (lax.axis_index("blk") ^ flip) * rows + lax.broadcasted_iota(jnp.int32, (rows, rows), 0)
     total = jnp.zeros(part.shape, jnp.float32)
     for block in images:
         products = rows_by_rows(texts[...], block[:rows, :])
-        slopes, _ = slopes_and_loss(products, temper, bias[...], index == labels_of(block, rows))
+        slopes, _ = slopes_and_loss(products, temper, settings[:, 1:2], index == labels_of(block, rows))
         total += jnp.dot(slopes, block[:rows, :], preferred_element_type=jnp.float32)
     part[...] = temper * total
 
@@ -159,7 +157,8 @@
     def grads(slopes, others):
         return temper * jnp.dot(slopes, others, preferred_element_type=jnp.float32)
 
-    packed = after(jnp.concatenate([images, texts]))
+    settings = jnp.concatenate([log_temp, bias]).reshape(1, 2)
+    packed = after(jnp.concatenate([images, texts]), settings)
     tailed = images.shape[0]
     own_images, own_texts = packed[:rows], packed[tailed:]
     hops = [("blk", blocks, 1)] + [("group", groups, 1 << step) for step in range(groups.bit_length() - 1)]
@@ -183,20 +182,26 @@
         text_three_off = along(after(text_two_off, text_one_off, mate, scorer_image), 2)
         image_two_off = along(scorer_image, 4)
         image_one_off = along(after(scorer_image, text_three_off), 2)
-        column_texts = [partner_text, text_two_off, text_one_off, after(text_three_off, image_two_off)]
-        scalars = (log_temp.reshape(1, 1), bias.reshape(1, 1))
-        block_shape = texts.shape
-        own_part, mate_part, total = call(
-            image_kernel, [*scalars, packed[:tailed], mate[:tailed], *column_texts], [block_shape, block_shape, (8, 128)], "image_side"
-        )
-        image_three_off = along(after(image_two_off, image_one_off, total), 2)
-        image_grads = own_part + along(mate_part, 1)
-        total = hop_sum(total, hops[:2])
+        column_texts = [partner_text, text_two_off, text_one_off, text_three_off]
+        grad_shape, loss_shape = texts.shape, (8, 128)
+        mate_part, mate_loss = call(image_kernel, [settings, mate[:tailed], *column_texts], [grad_shape, loss_shape], "image_side_mate")
+        image_two_off = along(scorer_image, 4)
+        image_one_off = along(after(scorer_image, text_three_off), 2)
+        image_three_off = along(after(image_two_off, mate_part), 2)
+        image_part = along(mate_part, 1)
+        own_images = after(packed[:tailed], image_two_off)
+        own_part, own_loss = call(image_kernel, [settings, own_images, *column_texts], [grad_shape, loss_shape], "image_side_own")
+        image_grads = own_part + image_part
+
+        total = hop_sum(after(mate_loss + own_loss, image_part), hops[:1])
+        total = hop_sum(after(total, image_one_off), hops[1:2])
         column_images = [scorer_image, image_two_off, image_one_off, after(image_three_off, total)]
-        mate_part = call(functools.partial(text_kernel, 1), [*scalars, mate[tailed:], *column_images], [block_shape], "text_side_mate")[0]
-        own_part = call(functools.partial(text_kernel, 0), [*scalars, own_texts, *column_images], [block_shape], "text_side_own")[0]
+        mate_part = call(functools.partial(text_kernel, 1), [settings, mate[tailed:], *column_images], [grad_shape], "text_side_mate")[0]
+        own_part = call(functools.partial(text_kernel, 0), [settings, own_texts, *column_images], [grad_shape], "text_side_own")[0]
         text_grads = own_part + along(mate_part, 1)
-        total = after(total, image_grads)
+        total = hop_sum(after(total, mate_part), hops[2:4])
+        total = after(total, own_part)
+        hops = hops[:2] + hops[4:]
     else:
         temper = jnp.exp(log_temp[0])
         offset = bias[0]
@@ -214,7 +219,7 @@
         text_grads = grads(back_slopes, all_images)
 
     total = hop_sum(total, hops[2:])
-    loss = jnp.sum(total).reshape(1) / (groups * rows * blocks * blocks)
+    loss = jnp.sum(total * (1.0 / (groups * rows * blocks * blocks))).reshape(1)
     return (image_grads[None], text_grads[None], loss)
 
 

time: 79.6 us -> 72.3 us (0.908)
  waiting for transfers between devices: 39.6 us -> 30.9 us
  starting transfers between devices: 17.4 us -> 20.2 us
  between operations: 3.85 us -> 2.1 us
    ppermute x16, waiting for transfers between devices: 39.6 us -> 30.9 us  [exchange(): lax.ppermute(array, axis, [(place, mate(place)) for place in range(size)])]
    ppermute x16, starting transfers between devices: 17.4 us -> 20.2 us  [exchange(): lax.ppermute(array, axis, [(place, mate(place)) for place in range(size)])]
    add x1, other arithmetic: 0.83 us -> 0.01 us  [shards(): total = hop_sum(after(mate_loss + own_loss, image_part), hops[:1])]
    broadcast_in_dim x1 -> x2, other arithmetic: 0.82 us -> 1.62 us  [shards(): return (image_grads[None], text_grads[None], loss)]
    pallas_call x6 -> x7, Pallas kernels: 5.26 us -> 5.42 us  [call(): pl.pallas_call(kernel, out_shape=[jax.ShapeDtypeStruct(shape, dtype) for...]
  transfers between devices with their start and end apart: 16 -> 16, of which waited for: 10 -> 10; matrix products, arithmetic and copies ran while one was open for 3% -> 4% of each run, Pallas kernels for 6% -> 6%
where the time goes in v1:
time: 72.3 us; the launch traced here: 72.1 us
  waiting for transfers between devices  30.9 us (43%)
  starting transfers between devices  20.2 us (28%)
  blocking collectives  9.92 us (14%)
  Pallas kernels  5.42 us (7%)
  other arithmetic  3.42 us (5%)
  between operations  2.1 us (3%)
    ppermute x16, waiting for transfers between devices, exchange(): lax.ppermute(array, axis, [(place, mate(place)) for place in range(size)])  30.9 us
    ppermute x16, starting transfers between devices, exchange(): lax.ppermute(array, axis, [(place, mate(place)) for place in range(size)])  20.2 us
    all_gather x1, blocking collectives, shards(): group_images = lax.all_gather(after(packed[:tailed], partner_text), 'group')  9.92 us
    pallas_call x7, Pallas kernels, call(): pl.pallas_call(kernel, out_shape=[jax.ShapeDtypeStruct(shape, dtype) for...  5.42 us
    broadcast_in_dim x2, other arithmetic, shards(): return (image_grads[None], text_grads[None], loss)  1.62 us
  transfers between devices with their start and end apart: 16, of which 10 were waited for; matrix products, arithmetic and copies ran while one was open for 4% of the time, Pallas kernels for 6%

profile of v1, /device:TPU:0, one launch (start us, length us, event | category | flops | bytes accessed | tf_op | source)
XLA Modules:
  0.0 72.1 jit_solution(2301568103881370098)
XLA Ops:
  0.6 3.0 %collective-permute-start = (bf16[96,1152]{1,0:T(8,128)(2,1)}, bf16[96,1152]{1,0:T(8,128)(2,1)S(1)}, u32[]{:S(2)}, u32[]{:S(2)}) collective-permute-start(bf16[96,1152]{1,0:T(8,128)(2,1)} %bitcast.16), channel_id=1, source_target_pairs={{0,2},{1,3},{2,0},{3,1},{4,6},{5,7},{6,4},{7,5},{8,10},{9,11},{10,... | collective-permute-start | bytes 663560 | tf_op jit(solution)/shard_map/ppermute | solution.py:22
  4.3 0.0 copy-start.1
  5.0 0.0 copy-done.1
  5.0 0.1 maximum_bitcast_fusion.settings
  5.1 1.1 %pad_maximum_fusion = bf16[208,1152]{1,0:T(8,128)(2,1)S(1)} fusion(bf16[96,1152]{1,0:T(8,128)(2,1)} %bitcast.17, bf16[16,1152]{1,0:T(8,128)(2,1)S(1)} %fusion.5, bf16[96,1152]{1,0:T(8,128)(2,1)} %bitcast.15), kind=kLoop, calls=%fused_computation | loop fusion | flops 1437696 | bytes 958464 | tf_op jit(solution)/shard_map/concatenate | solution.py:161
  6.2 0.0 copy-start
  6.2 3.1 %collective-permute-done.across = bf16[96,1152]{1,0:T(8,128)(2,1)S(1)} collective-permute-done((bf16[96,1152]{1,0:T(8,128)(2,1)}, bf16[96,1152]{1,0:T(8,128)(2,1)S(1)}, u32[]{:S(2)}, u32[]{:S(2)}) %collective-permute-start) | collective-permute-done | bytes 221216 | tf_op jit(solution)/shard_map/ppermute | solution.py:22
  9.3 0.1 offer.1
  9.4 0.1 collective-permute-start.1
  9.5 1.8 %collective-permute-start.5 = (bf16[208,1152]{1,0:T(8,128)(2,1)S(1)}, bf16[208,1152]{1,0:T(8,128)(2,1)S(1)}, u32[]{:S(2)}, u32[]{:S(2)}) collective-permute-start(bf16[208,1152]{1,0:T(8,128)(2,1)S(1)} %pad_maximum_fusion), channel_id=1, source_target_pairs={{0,4},{4,0},{8,12},{12,8},{16,20},{20,16},{24,28},{28,24},{1,5},{5... | collective-permute-start | bytes 1437704 | tf_op jit(solution)/shard_map/ppermute | solution.py:22
  11.3 0.0 collective-permute-done.1.offered
  11.3 0.1 choose.1.refs_0_
  11.5 2.7 %collective-permute-start.3 = (bf16[96,1152]{1,0:T(8,128)(2,1)S(1)}, bf16[96,1152]{1,0:T(8,128)(2,1)S(1)}, u32[]{:S(2)}, u32[]{:S(2)}) collective-permute-start(bf16[96,1152]{1,0:T(8,128)(2,1)S(1)} %choose.1.refs_0_), channel_id=1, source_target_pairs={{0,16},{4,20},{8,24},{12,28},{16,0},{20,4},{24,8},{28,12},{1,17},{... | collective-permute-start | bytes 663560 | tf_op jit(solution)/shard_map/ppermute | solution.py:22
  14.1 1.6 %collective-permute-start.4 = (bf16[96,1152]{1,0:T(8,128)(2,1)S(1)}, bf16[96,1152]{1,0:T(8,128)(2,1)S(1)}, u32[]{:S(2)}, u32[]{:S(2)}) collective-permute-start(bf16[96,1152]{1,0:T(8,128)(2,1)S(1)} %choose.1.refs_0_), channel_id=1, source_target_pairs={{0,8},{4,12},{8,0},{12,4},{16,24},{20,28},{24,16},{28,20},{1,9},{5... | collective-permute-start | bytes 663560 | tf_op jit(solution)/shard_map/ppermute | solution.py:22
  15.7 9.9 %all-gather = bf16[448,1152]{1,0:T(8,128)(2,1)S(1)} all-gather(bf16[112,1152]{1,0:T(8,128)(2,1)S(1)} %slice.13.images), channel_id=2, replica_groups=mesh['blk'=8,'group'=4] {'group'}, dimensions={0}, use_global_device_ids=true | all-gather | bytes 1290240 | tf_op jit(solution)/shard_map/all_gather | solution.py:171
  25.6 0.2 scorer.1.refs_0_
  25.8 0.0 collective-permute-done.5
  25.8 0.0 collective-permute-done.3.refs_1_
  25.8 0.0 collective-permute-done.4.refs_2_
  25.8 0.6 collective-permute-start.6
  26.4 2.3 %collective-permute-start.2 = (bf16[112,1152]{1,0:T(8,128)(2,1)S(1)}, bf16[112,1152]{1,0:T(8,128)(2,1)S(1)}, u32[]{:S(2)}, u32[]{:S(2)}) collective-permute-start(bf16[112,1152]{1,0:T(8,128)(2,1)S(1)} %scorer.1.refs_0_), channel_id=1, source_target_pairs={{0,16},{4,20},{8,24},{12,28},{16,0},{20,4},{24,8},{28,12},{1,17},{... | collective-permute-start | bytes 774152 | tf_op jit(solution)/shard_map/ppermute | solution.py:22
  28.8 8.8 %collective-permute-done.6.refs_3_ = bf16[96,1152]{1,0:T(8,128)(2,1)S(1)} collective-permute-done((bf16[96,1152]{1,0:T(8,128)(2,1)S(1)}, bf16[96,1152]{1,0:T(8,128)(2,1)S(1)}, u32[]{:S(2)}, u32[]{:S(2)}) %collective-permute-start.6) | collective-permute-done | bytes 221216 | tf_op jit(solution)/shard_map/ppermute | solution.py:22
  37.5 1.4 %image_side_mate.1 = (f32[96,1152]{1,0:T(8,128)S(1)}, f32[8,128]{1,0:T(8,128)S(1)}) custom-call(f32[1,2]{1,0:T(1,128)S(1)} %maximum_bitcast_fusion.settings, bf16[112,1152]{1,0:T(8,128)(2,1)S(1)} %slice.17.images, bf16[96,1152]{1,0:T(8,128)(2,1)S(1)} %choose.1.refs_0_, bf16[96,1152]{1,0:T(8,128)(2,1)S(1)} %collective-permute-done.3.refs_1_, ...), custom_call_target="tpu_custom_call" | custom-call | tf_op jit(solution)/shard_map/image_side_mate/pallas_call | solution.py:126
  38.9 1.4 %collective-permute-start.7 = (f32[96,1152]{1,0:T(8,128)S(1)}, f32[96,1152]{1,0:T(8,128)S(1)}, u32[]{:S(2)}, u32[]{:S(2)}) collective-permute-start(f32[96,1152]{1,0:T(8,128)S(1)} %get-tuple-element.23), channel_id=1, source_target_pairs={{0,4},{4,0},{8,12},{12,8},{16,20},{20,16},{24,28},{28,24},{1,5},{5... | collective-permute-start | bytes 1327112 | tf_op jit(solution)/shard_map/ppermute | solution.py:22
  40.3 0.0 collective-permute-start.8
  40.3 0.7 %collective-permute-done.2.refs_1_ = bf16[112,1152]{1,0:T(8,128)(2,1)S(1)} collective-permute-done((bf16[112,1152]{1,0:T(8,128)(2,1)S(1)}, bf16[112,1152]{1,0:T(8,128)(2,1)S(1)}, u32[]{:S(2)}, u32[]{:S(2)}) %collective-permute-start.2) | collective-permute-done | bytes 258080 | tf_op jit(solution)/shard_map/ppermute | solution.py:22
  41.0 1.3 %collective-permute-start.9 = (bf16[112,1152]{1,0:T(8,128)(2,1)S(1)}, bf16[112,1152]{1,0:T(8,128)(2,1)S(1)}, u32[]{:S(2)}, u32[]{:S(2)}) collective-permute-start(bf16[112,1152]{1,0:T(8,128)(2,1)S(1)} %collective-permute-done.2.refs_1_), channel_id=1, source_target_pairs={{0,8},{4,12},{8,0},{12,4},{16,24},{20,28},{24,16},{28,20},{1,9},{5... | collective-permute-start | bytes 774152 | tf_op jit(solution)/shard_map/ppermute | solution.py:22
  42.3 1.4 %image_side_own.1 = (f32[96,1152]{1,0:T(8,128)S(1)}, f32[8,128]{1,0:T(8,128)S(1)}) custom-call(f32[1,2]{1,0:T(1,128)S(1)} %maximum_bitcast_fusion.settings, bf16[112,1152]{1,0:T(8,128)(2,1)S(1)} %slice.13.images, bf16[96,1152]{1,0:T(8,128)(2,1)S(1)} %choose.1.refs_0_, bf16[96,1152]{1,0:T(8,128)(2,1)S(1)} %collective-permute-done.3.refs_1_, ...), custom_call_target="tpu_custom_call" | custom-call | tf_op jit(solution)/shard_map/image_side_own/pallas_call | solution.py:126
  43.7 6.9 %collective-permute-done.7 = f32[96,1152]{1,0:T(8,128)S(1)} collective-permute-done((f32[96,1152]{1,0:T(8,128)S(1)}, f32[96,1152]{1,0:T(8,128)S(1)}, u32[]{:S(2)}, u32[]{:S(2)}) %collective-permute-start.7) | collective-permute-done | bytes 442400 | tf_op jit(solution)/shard_map/ppermute | solution.py:22
  50.6 1.3 %collective-permute-start.10 = (f32[8,128]{1,0:T(8,128)S(1)}, f32[8,128]{1,0:T(8,128)S(1)}, u32[]{:S(2)}, u32[]{:S(2)}) collective-permute-start(f32[8,128]{1,0:T(8,128)S(1)} %add.37), channel_id=1, source_target_pairs={{0,4},{4,0},{8,12},{12,8},{16,20},{20,16},{24,28},{28,24},{1,5},{5... | collective-permute-start | bytes 12296 | tf_op jit(solution)/shard_map/ppermute | solution.py:22
  51.9 2.3 %collective-permute-done.10 = f32[8,128]{1,0:T(8,128)S(1)} collective-permute-done((f32[8,128]{1,0:T(8,128)S(1)}, f32[8,128]{1,0:T(8,128)S(1)}, u32[]{:S(2)}, u32[]{:S(2)}) %collective-permute-start.10) | collective-permute-done | bytes 4128 | tf_op jit(solution)/shard_map/ppermute | solution.py:22
  54.2 0.0 collective-permute-done.8.refs_2_
  54.2 0.0 collective-permute-start.11
  54.3 1.1 %collective-permute-done.11 = f32[8,128]{1,0:T(8,128)S(1)} collective-permute-done((f32[8,128]{1,0:T(8,128)S(1)}, f32[8,128]{1,0:T(8,128)S(1)}, u32[]{:S(2)}, u32[]{:S(2)}) %collective-permute-start.11) | collective-permute-done | bytes 4128 | tf_op jit(solution)/shard_map/ppermute | solution.py:22
  55.4 0.0 collective-permute-done.9.refs_3_
  55.4 1.1 %text_side_mate.1 = f32[96,1152]{1,0:T(8,128)S(1)} custom-call(f32[1,2]{1,0:T(1,128)S(1)} %maximum_bitcast_fusion.settings, bf16[96,1152]{1,0:T(8,128)(2,1)S(1)} %slice.18.texts, bf16[112,1152]{1,0:T(8,128)(2,1)S(1)} %scorer.1.refs_0_, bf16[112,1152]{1,0:T(8,128)(2,1)S(1)} %collective-permute-done.2.refs_1_, ...), custom_call_target="tpu_custom_call" | custom-call | tf_op jit(solution)/shard_map/text_side_mate/pallas_call | solution.py:126
  56.5 1.5 %collective-permute-start.13 = (f32[8,128]{1,0:T(8,128)S(1)}, f32[8,128]{1,0:T(8,128)S(1)}, u32[]{:S(2)}, u32[]{:S(2)}) collective-permute-start(f32[8,128]{1,0:T(8,128)S(1)} %add.39), channel_id=1, source_target_pairs={{0,2},{1,3},{2,0},{3,1},{4,6},{5,7},{6,4},{7,5},{8,10},{9,11},{10,... | collective-permute-start | bytes 12296 | tf_op jit(solution)/shard_map/ppermute | solution.py:22
  58.0 2.2 %collective-permute-done.13 = f32[8,128]{1,0:T(8,128)S(1)} collective-permute-done((f32[8,128]{1,0:T(8,128)S(1)}, f32[8,128]{1,0:T(8,128)S(1)}, u32[]{:S(2)}, u32[]{:S(2)}) %collective-permute-start.13) | collective-permute-done | bytes 4128 | tf_op jit(solution)/shard_map/ppermute | solution.py:22
  60.2 0.0 collective-permute-start.14
  60.2 1.3 %collective-permute-start.12 = (f32[96,1152]{1,0:T(8,128)S(1)}, f32[96,1152]{1,0:T(8,128)S(1)}, u32[]{:S(2)}, u32[]{:S(2)}) collective-permute-start(f32[96,1152]{1,0:T(8,128)S(1)} %text_side_mate.1), channel_id=1, source_target_pairs={{0,4},{4,0},{8,12},{12,8},{16,20},{20,16},{24,28},{28,24},{1,5},{5... | collective-permute-start | bytes 1327112 | tf_op jit(solution)/shard_map/ppermute | solution.py:22
  61.5 1.1 %text_side_own.1 = f32[96,1152]{1,0:T(8,128)S(1)} custom-call(f32[1,2]{1,0:T(1,128)S(1)} %maximum_bitcast_fusion.settings, bf16[96,1152]{1,0:T(8,128)(2,1)S(1)} %slice.14.own.texts, bf16[112,1152]{1,0:T(8,128)(2,1)S(1)} %scorer.1.refs_0_, bf16[112,1152]{1,0:T(8,128)(2,1)S(1)} %collective-permute-done.2.refs_1_, ...), custom_call_target="tpu_custom_call" | custom-call | tf_op jit(solution)/shard_map/text_side_own/pallas_call | solution.py:126
  62.7 1.1 %collective-permute-done.14 = f32[8,128]{1,0:T(8,128)S(1)} collective-permute-done((f32[8,128]{1,0:T(8,128)S(1)}, f32[8,128]{1,0:T(8,128)S(1)}, u32[]{:S(2)}, u32[]{:S(2)}) %collective-permute-start.14) | collective-permute-done | bytes 4128 | tf_op jit(solution)/shard_map/ppermute | solution.py:22
  63.8 1.4 %collective-permute-start.15 = (f32[8,128]{1,0:T(8,128)S(1)}, f32[8,128]{1,0:T(8,128)S(1)}, u32[]{:S(2)}, u32[]{:S(2)}) collective-permute-start(f32[8,128]{1,0:T(8,128)S(1)} %add.42), channel_id=1, source_target_pairs={{0,16},{4,20},{8,24},{12,28},{16,0},{20,4},{24,8},{28,12},{1,17},{... | collective-permute-start | bytes 12296 | tf_op jit(solution)/shard_map/ppermute | solution.py:22
  65.2 0.8 %add_bitcast_fusion.1 = f32[1,96,1152]{2,1,0:T(8,128)} fusion(f32[96,1152]{1,0:T(8,128)S(1)} %get-tuple-element.22, f32[96,1152]{1,0:T(8,128)S(1)} %collective-permute-done.7), kind=kLoop, calls=%fused_computation.2 | loop fusion | flops 110592 | bytes 1327104 | tf_op jit(solution)/shard_map/broadcast_in_dim | solution.py:223
  66.0 2.3 %collective-permute-done.15 = f32[8,128]{1,0:T(8,128)S(1)} collective-permute-done((f32[8,128]{1,0:T(8,128)S(1)}, f32[8,128]{1,0:T(8,128)S(1)}, u32[]{:S(2)}, u32[]{:S(2)}) %collective-permute-start.15) | collective-permute-done | bytes 4128 | tf_op jit(solution)/shard_map/ppermute | solution.py:22
  68.3 0.6 multiply_reduce_fusion
  68.9 2.4 %collective-permute-done.12 = f32[96,1152]{1,0:T(8,128)S(1)} collective-permute-done((f32[96,1152]{1,0:T(8,128)S(1)}, f32[96,1152]{1,0:T(8,128)S(1)}, u32[]{:S(2)}, u32[]{:S(2)}) %collective-permute-start.12) | collective-permute-done | bytes 442400 | tf_op jit(solution)/shard_map/ppermute | solution.py:22
  71.3 0.8 %add_bitcast_fusion = f32[1,96,1152]{2,1,0:T(8,128)} fusion(f32[96,1152]{1,0:T(8,128)S(1)} %text_side_own.1, f32[96,1152]{1,0:T(8,128)S(1)} %collective-permute-done.12), kind=kLoop, calls=%fused_computation.1 | loop fusion | flops 110592 | bytes 1327104 | tf_op jit(solution)/shard_map/broadcast_in_dim | solution.py:223
  (12 shorter events, 0.1 us)
Async XLA Ops:
  0.6 8.6 %collective-permute-start = (bf16[96,1152]{1,0:T(8,128)(2,1)}, bf16[96,1152]{1,0:T(8,128)(2,1)S(1)}, u32[]{:S(2)}, u32[]{:S(2)}) collective-permute-start(bf16[96,1152]{1,0:T(8,128)(2,1)} %bitcast.16), channel_id=1, source_target_pairs={{0,2},{1,3},{2,0},{3,1},{4,6},{5,7},{6,4},{7,5},{8,10},{9,11},{10,... | collective-permute-start | bytes 663560 | tf_op jit(solution)/shard_map/ppermute | solution.py:22
  4.3 0.7 copy-start.1
  6.2 3.1 %copy-start = (s32[4]{0:T(128)S(1)}, s32[4]{0:T(128)}, u32[]{:S(2)}) copy-start(s32[4]{0:T(128)} %param.9) | copy-start | bytes 52
  9.4 1.9 %collective-permute-start.1 = (bf16[96,1152]{1,0:T(8,128)(2,1)S(1)}, bf16[96,1152]{1,0:T(8,128)(2,1)S(1)}, u32[]{:S(2)}, u32[]{:S(2)}) collective-permute-start(bf16[96,1152]{1,0:T(8,128)(2,1)S(1)} %offer.1), channel_id=1, source_target_pairs={{0,1},{1,0},{2,3},{3,2},{4,5},{5,4},{6,7},{7,6},{8,9},{9,8},{10,11... | collective-permute-start | bytes 663560 | tf_op jit(solution)/shard_map/ppermute | solution.py:22
  9.5 16.3 %collective-permute-start.5 = (bf16[208,1152]{1,0:T(8,128)(2,1)S(1)}, bf16[208,1152]{1,0:T(8,128)(2,1)S(1)}, u32[]{:S(2)}, u32[]{:S(2)}) collective-permute-start(bf16[208,1152]{1,0:T(8,128)(2,1)S(1)} %pad_maximum_fusion), channel_id=1, source_target_pairs={{0,4},{4,0},{8,12},{12,8},{16,20},{20,16},{24,28},{28,24},{1,5},{5... | collective-permute-start | bytes 1437704 | tf_op jit(solution)/shard_map/ppermute | solution.py:22
  11.5 14.3 %collective-permute-start.3 = (bf16[96,1152]{1,0:T(8,128)(2,1)S(1)}, bf16[96,1152]{1,0:T(8,128)(2,1)S(1)}, u32[]{:S(2)}, u32[]{:S(2)}) collective-permute-start(bf16[96,1152]{1,0:T(8,128)(2,1)S(1)} %choose.1.refs_0_), channel_id=1, source_target_pairs={{0,16},{4,20},{8,24},{12,28},{16,0},{20,4},{24,8},{28,12},{1,17},{... | collective-permute-start | bytes 663560 | tf_op jit(solution)/shard_map/ppermute | solution.py:22
  14.1 11.7 %collective-permute-start.4 = (bf16[96,1152]{1,0:T(8,128)(2,1)S(1)}, bf16[96,1152]{1,0:T(8,128)(2,1)S(1)}, u32[]{:S(2)}, u32[]{:S(2)}) collective-permute-start(bf16[96,1152]{1,0:T(8,128)(2,1)S(1)} %choose.1.refs_0_), channel_id=1, source_target_pairs={{0,8},{4,12},{8,0},{12,4},{16,24},{20,28},{24,16},{28,20},{1,9},{5... | collective-permute-start | bytes 663560 | tf_op jit(solution)/shard_map/ppermute | solution.py:22
  25.8 11.7 %collective-permute-start.6 = (bf16[96,1152]{1,0:T(8,128)(2,1)S(1)}, bf16[96,1152]{1,0:T(8,128)(2,1)S(1)}, u32[]{:S(2)}, u32[]{:S(2)}) collective-permute-start(bf16[96,1152]{1,0:T(8,128)(2,1)S(1)} %collective-permute-done.3.refs_1_), channel_id=1, source_target_pairs={{0,8},{4,12},{8,0},{12,4},{16,24},{20,28},{24,16},{28,20},{1,9},{5... | collective-permute-start | bytes 663560 | tf_op jit(solution)/shard_map/ppermute | solution.py:22
  26.4 14.6 %collective-permute-start.2 = (bf16[112,1152]{1,0:T(8,128)(2,1)S(1)}, bf16[112,1152]{1,0:T(8,128)(2,1)S(1)}, u32[]{:S(2)}, u32[]{:S(2)}) collective-permute-start(bf16[112,1152]{1,0:T(8,128)(2,1)S(1)} %scorer.1.refs_0_), channel_id=1, source_target_pairs={{0,16},{4,20},{8,24},{12,28},{16,0},{20,4},{24,8},{28,12},{1,17},{... | collective-permute-start | bytes 774152 | tf_op jit(solution)/shard_map/ppermute | solution.py:22
  38.9 11.7 %collective-permute-start.7 = (f32[96,1152]{1,0:T(8,128)S(1)}, f32[96,1152]{1,0:T(8,128)S(1)}, u32[]{:S(2)}, u32[]{:S(2)}) collective-permute-start(f32[96,1152]{1,0:T(8,128)S(1)} %get-tuple-element.23), channel_id=1, source_target_pairs={{0,4},{4,0},{8,12},{12,8},{16,20},{20,16},{24,28},{28,24},{1,5},{5... | collective-permute-start | bytes 1327112 | tf_op jit(solution)/shard_map/ppermute | solution.py:22
  40.3 13.9 %collective-permute-start.8 = (bf16[112,1152]{1,0:T(8,128)(2,1)S(1)}, bf16[112,1152]{1,0:T(8,128)(2,1)S(1)}, u32[]{:S(2)}, u32[]{:S(2)}) collective-permute-start(bf16[112,1152]{1,0:T(8,128)(2,1)S(1)} %scorer.1.refs_0_), channel_id=1, source_target_pairs={{0,8},{4,12},{8,0},{12,4},{16,24},{20,28},{24,16},{28,20},{1,9},{5... | collective-permute-start | bytes 774152 | tf_op jit(solution)/shard_map/ppermute | solution.py:22
  41.0 14.4 %collective-permute-start.9 = (bf16[112,1152]{1,0:T(8,128)(2,1)S(1)}, bf16[112,1152]{1,0:T(8,128)(2,1)S(1)}, u32[]{:S(2)}, u32[]{:S(2)}) collective-permute-start(bf16[112,1152]{1,0:T(8,128)(2,1)S(1)} %collective-permute-done.2.refs_1_), channel_id=1, source_target_pairs={{0,8},{4,12},{8,0},{12,4},{16,24},{20,28},{24,16},{28,20},{1,9},{5... | collective-permute-start | bytes 774152 | tf_op jit(solution)/shard_map/ppermute | solution.py:22
  50.6 3.6 %collective-permute-start.10 = (f32[8,128]{1,0:T(8,128)S(1)}, f32[8,128]{1,0:T(8,128)S(1)}, u32[]{:S(2)}, u32[]{:S(2)}) collective-permute-start(f32[8,128]{1,0:T(8,128)S(1)} %add.37), channel_id=1, source_target_pairs={{0,4},{4,0},{8,12},{12,8},{16,20},{20,16},{24,28},{28,24},{1,5},{5... | collective-permute-start | bytes 12296 | tf_op jit(solution)/shard_map/ppermute | solution.py:22
  54.2 1.2 %collective-permute-start.11 = (f32[8,128]{1,0:T(8,128)S(1)}, f32[8,128]{1,0:T(8,128)S(1)}, u32[]{:S(2)}, u32[]{:S(2)}) collective-permute-start(f32[8,128]{1,0:T(8,128)S(1)} %add.38), channel_id=1, source_target_pairs={{0,1},{1,0},{2,3},{3,2},{4,5},{5,4},{6,7},{7,6},{8,9},{9,8},{10,11... | collective-permute-start | bytes 12296 | tf_op jit(solution)/shard_map/ppermute | solution.py:22
  56.5 3.7 %collective-permute-start.13 = (f32[8,128]{1,0:T(8,128)S(1)}, f32[8,128]{1,0:T(8,128)S(1)}, u32[]{:S(2)}, u32[]{:S(2)}) collective-permute-start(f32[8,128]{1,0:T(8,128)S(1)} %add.39), channel_id=1, source_target_pairs={{0,2},{1,3},{2,0},{3,1},{4,6},{5,7},{6,4},{7,5},{8,10},{9,11},{10,... | collective-permute-start | bytes 12296 | tf_op jit(solution)/shard_map/ppermute | solution.py:22
  60.2 3.6 %collective-permute-start.14 = (f32[8,128]{1,0:T(8,128)S(1)}, f32[8,128]{1,0:T(8,128)S(1)}, u32[]{:S(2)}, u32[]{:S(2)}) collective-permute-start(f32[8,128]{1,0:T(8,128)S(1)} %add.41), channel_id=1, source_target_pairs={{0,8},{4,12},{8,0},{12,4},{16,24},{20,28},{24,16},{28,20},{1,9},{5... | collective-permute-start | bytes 12296 | tf_op jit(solution)/shard_map/ppermute | solution.py:22
  60.2 11.1 %collective-permute-start.12 = (f32[96,1152]{1,0:T(8,128)S(1)}, f32[96,1152]{1,0:T(8,128)S(1)}, u32[]{:S(2)}, u32[]{:S(2)}) collective-permute-start(f32[96,1152]{1,0:T(8,128)S(1)} %text_side_mate.1), channel_id=1, source_target_pairs={{0,4},{4,0},{8,12},{12,8},{16,20},{20,16},{24,28},{28,24},{1,5},{5... | collective-permute-start | bytes 1327112 | tf_op jit(solution)/shard_map/ppermute | solution.py:22
  63.8 4.5 %collective-permute-start.15 = (f32[8,128]{1,0:T(8,128)S(1)}, f32[8,128]{1,0:T(8,128)S(1)}, u32[]{:S(2)}, u32[]{:S(2)}) collective-permute-start(f32[8,128]{1,0:T(8,128)S(1)} %add.42), channel_id=1, source_target_pairs={{0,16},{4,20},{8,24},{12,28},{16,0},{20,4},{24,8},{28,12},{1,17},{... | collective-permute-start | bytes 12296 | tf_op jit(solution)/shard_map/ppermute | solution.py:22
